TPU v7x, 32 devices: a whole 2x2x4 slice. The times are simulated.
32 devices in a mesh: batch: 16 (over z, x, core), blk: 2 (over y).
Axes of the slice: x: 2, y: 2, z: 4, core: 2. Of those that a mesh axis runs over, the one named last changes fastest.
Arguments:
- inputs: bfloat16 [32, 1024, 768], P('batch', 'blk'), may hold values from -6 to 6
- first_values: bfloat16 [32, 1024, 384], P('batch', 'blk'), may hold values from -6 to 6
- segments: int32 [32, 1024], P('batch', 'blk'), may hold values from -1 to 3, as said below
- ln1_gain: bfloat16 [768], replicated, may hold values from 0.5 to 1.5
- first_norm_bias: bfloat16 [768], replicated, may hold values from -3 to 3
- w_qkv: bfloat16 [768, 1920], replicated, may hold values from -0.21875 to 0.21875
- b_query: bfloat16 [768], replicated, may hold values from -3 to 3
- b_value: bfloat16 [384], replicated, may hold values from -3 to 3
- w_out: bfloat16 [768, 768], replicated, may hold values from -0.875 to 0.875
- b_out: bfloat16 [768], replicated, may hold values from -3 to 3
- ln2_gain: bfloat16 [768], replicated, may hold values from 0.5 to 1.5
- second_norm_bias: bfloat16 [768], replicated, may hold values from -3 to 3
- w_fc: bfloat16 [768, 3072], replicated, may hold values from -0.21875 to 0.21875
- b_fc: bfloat16 [3072], replicated, may hold values from -3 to 3
- w_proj: bfloat16 [3072, 768], replicated, may hold values from -0.109375 to 0.109375
- b_proj: bfloat16 [768], replicated, may hold values from -3 to 3
- cotangent: bfloat16 [32, 1024, 768], P('batch', 'blk'), may hold values from -6 to 6
Outputs:
- layer_out: bfloat16 [32, 1024, 768], P('batch', 'blk')
- grad_inputs: bfloat16 [32, 1024, 768], P('batch', 'blk')
- grad_first: bfloat16 [32, 1024, 384], P('batch', 'blk')
- grad_ln1_gain: float32 [768], P('batch')
- grad_ln1_bias: float32 [768], P('batch')
- grad_w_qkv: float32 [768, 1920], P('batch')
- grad_b_query: float32 [768], P('batch')
- grad_b_value: float32 [384], P('batch')
- grad_w_out: float32 [768, 768], P('batch')
- grad_b_out: float32 [768], P('batch')
- grad_ln2_gain: float32 [768], P('batch')
- grad_ln2_bias: float32 [768], P('batch')
- grad_w_fc: float32 [768, 3072], P('batch')
- grad_b_fc: float32 [3072], P('batch')
- grad_w_proj: float32 [3072, 768], P('batch')
- grad_b_proj: float32 [768], P('batch')
Inputs may be any that keep to these rules, and one draw needn't show every extreme that they name: `segments`: along each row the document numbers never fall before the padding; padding tokens carry -1 and form the row's tail.
All inputs are finite; a program needn't handle non-finite values.
Results may differ from a plain program's by a relative error of at most 0.02.
Values may be sent and summed in bfloat16 or wider, within the bound.
A program may use at most 320 MiB of HBM per device.

v0:
```python
import jax
import jax.numpy as jnp
from jax import lax
from jax.sharding import PartitionSpec as P

HEADS = 12
HEAD_DIM = 64
MICRO = 2


EPS = 1e-05
NEG = -1e30


def as_sent(shard):
    return jax.tree.map(lambda a: a.astype(jnp.bfloat16) if a.dtype == jnp.float32 else a, shard)


def apply_norm(values_in, norm_gain, shift_bias):
    mean_val = jnp.mean(values_in, axis=-1, keepdims=True)
    centred_rows = values_in - mean_val
    inverse_deviation = lax.rsqrt(
        jnp.mean(centred_rows * centred_rows, axis=-1, keepdims=True) + EPS
    )
    standardized = centred_rows * inverse_deviation
    return (standardized * norm_gain + shift_bias, standardized, inverse_deviation)


def apply_norm_backward(upstream_gradient, standardized, inverse_deviation, norm_gain):
    scaled_rows = upstream_gradient * norm_gain
    first_average = jnp.mean(scaled_rows, axis=-1, keepdims=True)
    second_average = jnp.mean(scaled_rows * standardized, axis=-1, keepdims=True)
    incoming_gradient = inverse_deviation * (
        scaled_rows - first_average - standardized * second_average
    )
    return (
        incoming_gradient,
        jnp.sum(upstream_gradient * standardized, axis=(0, 1)),
        jnp.sum(upstream_gradient, axis=(0, 1)),
    )


def gelu_tanh(values_in):
    cubic = values_in + 0.044715 * values_in * values_in * values_in
    return 0.5 * values_in * (1.0 + jnp.tanh(0.7978845608028654 * cubic))


def heads_of(values_in):
    return values_in.reshape(values_in.shape[0], values_in.shape[1], HEADS, HEAD_DIM)


def visible(seg_query, seg_key, query_pos, key_pos):
    same = seg_query[:, :, None] == seg_key[:, None, :]
    causal = key_pos[None, :] <= query_pos[:, None]
    live = seg_query[:, :, None] >= 0
    diagonal = key_pos[None, :] == query_pos[:, None]
    return (same & causal[None] & live | diagonal[None])[:, :, None, :]


def score_block(query4, key4, mask):
    raw = jnp.einsum("rqhd,rkhd->rqhk", query4, key4, preferred_element_type=jnp.float32)
    return jnp.where(mask, raw * HEAD_DIM ** (-0.5), NEG)


def grad_block(query4, key4, value4, dout4, log_total, out_dot, mask):
    probs = jnp.where(mask, jnp.exp(score_block(query4, key4, mask) - log_total[..., None]), 0.0)
    probs_low = probs.astype(jnp.bfloat16)
    grad_probs = jnp.einsum("rqhd,rkhd->rqhk", dout4, value4, preferred_element_type=jnp.float32)
    grad_scores = (probs * (grad_probs - out_dot[..., None]) * HEAD_DIM ** (-0.5)).astype(
        jnp.bfloat16
    )
    return (probs_low, grad_scores)


def local(
    inputs,
    first_values,
    segments,
    ln1_gain,
    first_norm_bias,
    w_qkv,
    b_query,
    b_value,
    w_out,
    b_out,
    ln2_gain,
    second_norm_bias,
    w_fc,
    b_fc,
    w_proj,
    b_proj,
    cotangent,
):
    all_seg = lax.all_gather(segments, "blk", axis=1, tiled=True)
    block_len = inputs.shape[1]
    model_width = inputs.shape[2]
    val_width = first_values.shape[2]
    rows_mb = inputs.shape[0] // MICRO
    own_pos = lax.axis_index("blk") * block_len + jnp.arange(block_len)
    first_gain = ln1_gain.astype(jnp.float32)
    second_gain = ln2_gain.astype(jnp.float32)
    outputs = []
    input_grads = []
    first_grads = []
    totals = None
    for micro_step in range(MICRO):
        first_row = micro_step * rows_mb
        last_row = first_row + rows_mb
        residual_stream = inputs[first_row:last_row].astype(jnp.float32)
        first_part = first_values[first_row:last_row]
        seg_local = segments[first_row:last_row]
        seg_row = all_seg[first_row:last_row]
        cot_part = cotangent[first_row:last_row]
        first_normed_rows, first_standardized, first_inverse_deviation = apply_norm(
            residual_stream, first_gain, first_norm_bias.astype(jnp.float32)
        )
        act1 = first_normed_rows.astype(jnp.bfloat16)
        projected = jnp.einsum("rbd,de->rbe", act1, w_qkv, preferred_element_type=jnp.float32)
        queries = (projected[..., :model_width] + b_query.astype(jnp.float32)).astype(jnp.bfloat16)
        keys_low = projected[..., model_width : 2 * model_width].astype(jnp.bfloat16)
        fresh = (projected[..., 2 * model_width :] + b_value.astype(jnp.float32)).astype(
            jnp.bfloat16
        )
        values_low = jnp.concatenate([fresh, first_part], axis=-1)
        query4 = heads_of(queries)
        key_part = lax.all_gather(keys_low, "blk", axis=1, tiled=True)
        value_part = lax.all_gather(values_low, "blk", axis=1, tiled=True)
        span = key_part.shape[1]
        key_pos = jnp.arange(span)
        mask = visible(seg_local, seg_row, own_pos, key_pos)
        scores = score_block(query4, heads_of(key_part), mask)
        old_max = jnp.full((rows_mb, block_len, HEADS), NEG, jnp.float32)
        new_max = jnp.maximum(old_max, jnp.max(scores, axis=-1))
        weights = jnp.where(mask, jnp.exp(scores - new_max[..., None]), 0.0)
        new_sum = jnp.sum(weights, axis=-1)
        new_acc = jnp.einsum(
            "rqhk,rkhd->rqhd",
            weights.astype(jnp.bfloat16),
            heads_of(value_part),
            preferred_element_type=jnp.float32,
        )
        attention4 = new_acc / new_sum[..., None]
        log_total = new_max + jnp.log(new_sum)
        attention_low = attention4.reshape(rows_mb, block_len, model_width).astype(jnp.bfloat16)
        branch = jnp.einsum("rbd,de->rbe", attention_low, w_out, preferred_element_type=jnp.float32)
        middle_state = residual_stream + branch + b_out.astype(jnp.float32)
        second_normed_rows, second_standardized, second_inverse_deviation = apply_norm(
            middle_state, second_gain, second_norm_bias.astype(jnp.float32)
        )
        act2 = second_normed_rows.astype(jnp.bfloat16)
        pre_gelu = jnp.einsum(
            "rbd,df->rbf", act2, w_fc, preferred_element_type=jnp.float32
        ) + b_fc.astype(jnp.float32)
        hidden = gelu_tanh(pre_gelu).astype(jnp.bfloat16)
        result = middle_state + jnp.einsum(
            "rbf,fd->rbd", hidden, w_proj, preferred_element_type=jnp.float32
        )
        result = result + b_proj.astype(jnp.float32)
        outputs.append(result.astype(jnp.bfloat16))
        upstream_gradient = cot_part.astype(jnp.float32)
        grad_wproj = jnp.einsum("rbf,rbd->fd", hidden, cot_part, preferred_element_type=jnp.float32)
        grad_bproj = jnp.sum(upstream_gradient, axis=(0, 1))
        grad_hidden = jnp.einsum(
            "rbd,fd->rbf", cot_part, w_proj, preferred_element_type=jnp.float32
        )
        gelu_value, gelu_pull = jax.vjp(gelu_tanh, pre_gelu)
        grad_pre = gelu_pull(grad_hidden)[0].astype(jnp.bfloat16)
        grad_wfc = jnp.einsum("rbd,rbf->df", act2, grad_pre, preferred_element_type=jnp.float32)
        grad_bfc = jnp.sum(grad_pre.astype(jnp.float32), axis=(0, 1))
        second_activation_gradient = jnp.einsum(
            "rbf,df->rbd", grad_pre, w_fc, preferred_element_type=jnp.float32
        )
        second_norm_gradient, second_gain_gradient, second_bias_gradient = apply_norm_backward(
            second_activation_gradient, second_standardized, second_inverse_deviation, second_gain
        )
        grad_middle = upstream_gradient + second_norm_gradient
        grad_branch = grad_middle.astype(jnp.bfloat16)
        grad_wout = jnp.einsum(
            "rbd,rbe->de", attention_low, grad_branch, preferred_element_type=jnp.float32
        )
        grad_bout = jnp.sum(grad_branch.astype(jnp.float32), axis=(0, 1))
        grad_attention = jnp.einsum(
            "rbe,de->rbd", grad_branch, w_out, preferred_element_type=jnp.float32
        ).astype(jnp.bfloat16)
        dout4 = heads_of(grad_attention)
        out_dot = jnp.sum(dout4.astype(jnp.float32) * attention4, axis=-1)
        back_key_part = lax.all_gather(keys_low, "blk", axis=1, tiled=True)
        back_value_part = lax.all_gather(values_low, "blk", axis=1, tiled=True)
        back_span = back_key_part.shape[1]
        back_key_pos = jnp.arange(back_span)
        back_mask = visible(seg_local, seg_row, own_pos, back_key_pos)
        part_key4 = heads_of(back_key_part)
        probs_low, grad_scores = grad_block(
            query4, part_key4, heads_of(back_value_part), dout4, log_total, out_dot, back_mask
        )
        query_acc = jnp.einsum(
            "rqhk,rkhd->rqhd", grad_scores, part_key4, preferred_element_type=jnp.float32
        )
        key_piece = jnp.einsum(
            "rqhk,rqhd->rkhd", grad_scores, query4, preferred_element_type=jnp.float32
        ).reshape(rows_mb, back_span, model_width)
        value_piece = jnp.einsum(
            "rqhk,rqhd->rkhd", probs_low, dout4, preferred_element_type=jnp.float32
        ).reshape(rows_mb, back_span, model_width)
        query_acc, key_acc, value_acc = (query_acc, key_piece, value_piece)
        grad_keys, grad_values = (
            lax.psum_scatter(
                key_acc.astype(jnp.bfloat16), "blk", scatter_dimension=1, tiled=True
            ).astype(jnp.float32),
            lax.psum_scatter(
                value_acc.astype(jnp.bfloat16), "blk", scatter_dimension=1, tiled=True
            ).astype(jnp.float32),
        )
        grad_query = query_acc.reshape(rows_mb, block_len, model_width)
        grad_qkv = jnp.concatenate(
            [
                grad_query.astype(jnp.bfloat16),
                grad_keys.astype(jnp.bfloat16),
                grad_values[..., :val_width].astype(jnp.bfloat16),
            ],
            axis=-1,
        )
        first_grads.append(grad_values[..., val_width:].astype(jnp.bfloat16))
        grad_wqkv = jnp.einsum("rbd,rbe->de", act1, grad_qkv, preferred_element_type=jnp.float32)
        grad_bquery = jnp.sum(grad_qkv[..., :model_width].astype(jnp.float32), axis=(0, 1))
        grad_bvalue = jnp.sum(grad_qkv[..., 2 * model_width :].astype(jnp.float32), axis=(0, 1))
        first_activation_gradient = jnp.einsum(
            "rbe,de->rbd", grad_qkv, w_qkv, preferred_element_type=jnp.float32
        )
        first_norm_gradient, first_gain_gradient, first_bias_gradient = apply_norm_backward(
            first_activation_gradient, first_standardized, first_inverse_deviation, first_gain
        )
        input_grads.append((grad_middle + first_norm_gradient).astype(jnp.bfloat16))
        gradient_set = (
            first_gain_gradient,
            first_bias_gradient,
            grad_wqkv,
            grad_bquery,
            grad_bvalue,
            grad_wout,
            grad_bout,
            second_gain_gradient,
            second_bias_gradient,
            grad_wfc,
            grad_bfc,
            grad_wproj,
            grad_bproj,
        )
        if totals is None:
            totals = gradient_set
        else:
            totals = tuple((older + newer for older, newer in zip(totals, gradient_set)))
    totals = jax.tree.map(
        lambda part: part.astype(jnp.float32),
        lax.psum_scatter(as_sent(totals), "batch", scatter_dimension=0, tiled=True),
    )
    totals = jax.tree.map(lambda part: part.astype(jnp.float32), lax.psum(as_sent(totals), "blk"))
    return (
        jnp.concatenate(outputs, axis=0),
        jnp.concatenate(input_grads, axis=0),
        jnp.concatenate(first_grads, axis=0),
    ) + tuple(totals)


def solution(mesh):
    placed = (
        P("batch", "blk", None),
        P("batch", "blk", None),
        P("batch", "blk"),
        P(),
        P(),
        P(),
        P(),
        P(),
        P(),
        P(),
        P(),
        P(),
        P(),
        P(),
        P(),
        P(),
        P("batch", "blk", None),
    )
    return jax.shard_map(
        local,
        mesh=mesh,
        in_specs=placed,
        out_specs=(
            P("batch", "blk", None),
            P("batch", "blk", None),
            P("batch", "blk", None),
            P("batch"),
            P("batch"),
            P("batch", None),
            P("batch"),
            P("batch"),
            P("batch", None),
            P("batch"),
            P("batch"),
            P("batch"),
            P("batch", None),
            P("batch"),
            P("batch", None),
            P("batch"),
        ),
        check_vma=False,
    )
```

profile of v0, /device:TPU:0, one launch (start us, length us, event | category | flops | bytes accessed | tf_op | source)
XLA Modules:
  0.0 664.0 jit_solution(16937541795802087856)
XLA Ops:
  17.2 3.0 convolution_bitcast_fusion
  22.1 2.0 fusion.116
  25.3 2.5 slice.152
  27.9 2.0 pad_maximum_fusion.3
  29.9 5.5 all_gather.20
  35.4 3.3 fusion.93
  38.7 2.3 copy.87
  42.3 2.3 copy.91
  44.6 2.1 fusion.49
  46.8 2.6 copy.86
  49.4 14.3 %fusion.12 = (f32[512,12]{0,1:T(8,128)S(1)}, f32[12,1024,512]{2,1,0:T(8,128)}) fusion(pred[512,1024]{0,1:T(8,128)(4,1)} %get-tuple-element.92, bf16[1024,12,64]{0,2,1:T(8,128)(2,1)} %bitcast.323, bf16[512,12,64]{0,2,1:T(8,128)(2,1)} %bitcast.329), kind=kOutput, calls=%fused_computation.20 | convolution fusion | flops 824174592 | bytes 28073984 | tf_op jit(solution)/shard_map/rqhd,rkhd->rqhk/dot_general | solution.py:61
  63.7 11.5 %fusion.6 = f32[512,12]{0,1:T(8,128)S(1)} fusion(f32[12,1024,512]{2,1,0:T(8,128)} %get-tuple-element.103, f32[512,12]{0,1:T(8,128)S(1)} %broadcast_maximum_fusion.1, pred[512,1024]{0,1:T(8,128)(4,1)S(1)} %copy-done.15), kind=kLoop, calls=%fused_computation.14 | loop fusion | flops 31451136 | bytes 25739264 | tf_op jit(solution)/shard_map/reduce_sum | solution.py:135
  75.8 2.6 copy.85
  78.4 13.8 %fusion.183 = (bf16[1,512,12,64]{1,3,2,0:T(8,128)(2,1)S(1)}, f32[1,512,12,64]{1,3,2,0:T(8,128)}) fusion(f32[512,12]{0,1:T(8,128)S(1)} %fusion.6, bf16[1024,12,64]{0,2,1:T(8,128)(2,1)} %bitcast.335, f32[12,1024,512]{2,1,0:T(8,128)} %get-tuple-element.103, f32[512,12]{0,1:T(8,128)S(1)} %broadcast_maximum_fusion.1, pred[512,1024]{0,1:T(8,128)(4,1)} %get-tuple-element.92), kind=kOutput, calls=%fused_computation.270 | convolution fusion | flops 837550080 | bytes 29671424 | tf_op jit(solution)/shard_map/rqhk,rkhd->rqhd/dot_general | solution.py:136
  94.7 9.5 %all-gather.11.cloned.1.call-done = bf16[1,1024,768]{2,1,0:T(8,128)(2,1)} async-done(((bf16[1,512,768]{2,1,0:T(8,128)(2,1)}), bf16[1,1024,768]{2,1,0:T(8,128)(2,1)}) %all-gather.11.cloned.1.call-update) | async-done | bytes 1572880 | tf_op jit(solution)/shard_map/all_gather | solution.py:126
  104.2 2.8 copy.90
  107.0 14.2 %fusion.13 = (f32[512,12]{0,1:T(8,128)S(1)}, f32[12,1024,512]{2,1,0:T(8,128)}) fusion(pred[512,1024]{0,1:T(8,128)(4,1)S(1)} %get-tuple-element.93, bf16[1024,12,64]{0,2,1:T(8,128)(2,1)} %bitcast.325, bf16[512,12,64]{0,2,1:T(8,128)(2,1)} %bitcast.327), kind=kOutput, calls=%fused_computation.21 | convolution fusion | flops 824174592 | bytes 28073984 | tf_op jit(solution)/shard_map/rqhd,rkhd->rqhk/dot_general | solution.py:61
  121.8 11.4 %fusion.8 = f32[512,12]{0,1:T(8,128)S(1)} fusion(f32[12,1024,512]{2,1,0:T(8,128)} %get-tuple-element.97, f32[512,12]{0,1:T(8,128)S(1)} %broadcast_maximum_fusion, pred[512,1024]{0,1:T(8,128)(4,1)S(1)} %get-tuple-element.93), kind=kLoop, calls=%fused_computation.16 | loop fusion | flops 31451136 | bytes 25739264 | tf_op jit(solution)/shard_map/reduce_sum | solution.py:135
  133.2 2.6 copy.89
  135.8 12.6 %fusion.181 = (bf16[1,512,12,64]{1,3,2,0:T(8,128)(2,1)S(1)}, f32[1,512,12,64]{1,3,2,0:T(8,128)}) fusion(f32[512,12]{0,1:T(8,128)S(1)} %fusion.8, bf16[1024,12,64]{0,2,1:T(8,128)(2,1)} %bitcast.337, f32[12,1024,512]{2,1,0:T(8,128)} %get-tuple-element.97, f32[512,12]{0,1:T(8,128)} %copy-done.30, pred[512,1024]{0,1:T(8,128)(4,1)S(1)} %get-tuple-element.93), kind=kOutput, calls=%fused_computation.268 | convolution fusion | flops 837550080 | bytes 29671424 | tf_op jit(solution)/shard_map/rqhk,rkhd->rqhd/dot_general | solution.py:136
  150.2 8.3 %fusion.166 = f32[512,3072]{1,0:T(8,128)} fusion(bf16[768,3072]{1,0:T(8,128)(2,1)} %param.29, f32[1,512,768]{2,1,0:T(8,128)S(1)} %copy-done.9, f32[768]{0:T(1024)S(1)} %copy-done.61, f32[768]{0:T(1024)S(1)} %convert_element_type.475, f32[512]{0:T(512)S(1)} %add_rsqrt_fusion.2, f32[512]{0:T(512)S(1)} %broadcast_multiply_fusion.10), kind=kOutput, calls=%fused_computation.258 | convolution fusion | flops 2417885184 | bytes 12593152 | tf_op jit(solution)/shard_map/rbd,df->rbf/dot_general | solution.py:151
  158.5 2.7 fusion.162
  161.3 12.3 %convert_reduce_fusion.1 = (f32[3072]{0:T(1024)}, bf16[512,3072]{1,0:T(8,128)(2,1)}) fusion(f32[512,3072]{1,0:T(8,128)} %fusion.166, f32[3072]{0:T(1024)S(1)} %copy-done.48, bf16[3072,768]{1,0:T(8,128)(2,1)S(1)} %bitcast.362, bf16[2,512,768]{2,1,0:T(8,128)(2,1)S(1)} %copy-done.20), kind=kOutput, calls=%fused_computation.59 | convolution fusion | flops 2458383360 | bytes 14966784 | tf_op jit(solution)/shard_map/rbd,fd->rbf/dot_general | solution.py:163
  173.6 8.0 %convert_reduce_fusion = (f32[3072]{0:T(1024)}, bf16[512,3072]{1,0:T(8,128)(2,1)S(1)}) fusion(f32[512,3072]{1,0:T(8,128)S(1)} %fusion.162, f32[3072]{0:T(1024)S(1)} %copy-done.48, bf16[3072,768]{1,0:T(8,128)(2,1)S(1)} %bitcast.362, bf16[2,512,768]{2,1,0:T(8,128)(2,1)S(1)} %copy-done.20), kind=kOutput, calls=%fused_computation.58 | convolution fusion | flops 2458383360 | bytes 14966784 | tf_op jit(solution)/shard_map/rbd,fd->rbf/dot_general | solution.py:163
  181.6 2.6 fusion.185
  184.7 3.7 fusion.95
  189.4 3.2 convert_reduce_fusion.4
  195.5 2.3 copy.93
  197.8 12.7 %fusion.69 = bf16[12,64,1024]{2,1,0:T(8,128)(2,1)} fusion(bf16[512,12,64]{0,2,1:T(8,128)(2,1)} %bitcast.349, f32[12,1024,512]{2,1,0:T(8,128)} %get-tuple-element.103, f32[512,12]{0,1:T(8,128)} %log_add_fusion.1, pred[512,1024]{0,1:T(8,128)(4,1)} %get-tuple-element.92), kind=kOutput, calls=%fused_computation.103 | convolution fusion | flops 837550080 | bytes 28073984 | tf_op jit(solution)/shard_map/rqhk,rqhd->rkhd/dot_general | solution.py:202
  210.5 2.6 copy.98
  213.2 2.5 copy.94
  215.7 3.4 convolution_convert_fusion.2
  219.1 2.9 copy.101
  222.0 2.3 copy.100
  224.3 12.8 %fusion.66 = bf16[12,64,1024]{2,1,0:T(8,128)(2,1)} fusion(bf16[512,12,64]{0,2,1:T(8,128)(2,1)} %bitcast.347, f32[12,1024,512]{2,1,0:T(8,128)} %get-tuple-element.97, f32[512,12]{0,1:T(8,128)S(1)} %log_add_fusion, pred[512,1024]{0,1:T(8,128)(4,1)S(1)} %get-tuple-element.93), kind=kOutput, calls=%fused_computation.102 | convolution fusion | flops 837550080 | bytes 28073984 | tf_op jit(solution)/shard_map/rqhk,rqhd->rkhd/dot_general | solution.py:202
  237.2 2.6 copy.105
  239.8 2.3 multiply_reduce_fusion.1
  242.1 16.9 %fusion.18 = bf16[512,12,1024]{0,2,1:T(8,128)(2,1)} fusion(f32[12,1024,512]{2,1,0:T(8,128)} %get-tuple-element.103, f32[512,12]{0,1:T(8,128)S(1)} %multiply_reduce_fusion.1, f32[512,12]{0,1:T(8,128)S(1)} %copy-done.34, pred[512,1024]{0,1:T(8,128)(4,1)} %get-tuple-element.92, bf16[1024,12,64]{0,2,1:T(8,128)(2,1)} %bitcast.336, bf16[512,12,64]{0,2,1:T(8,128)(2,1)} %bitcast.350), kind=kOutput, calls=%fused_computation.26 | convolution fusion | flops 855638016 | bytes 40681472 | tf_op jit(solution)/shard_map/rqhd,rkhd->rqhk/dot_general | solution.py:68
  259.1 10.0 %convolution_convert_fusion.1 = bf16[12,64,1024]{2,1,0:T(8,128)(2,1)} fusion(bf16[512,12,64]{0,2,1:T(8,128)(2,1)} %bitcast.330, bf16[512,12,1024]{0,2,1:T(8,128)(2,1)} %fusion.18), kind=kOutput, calls=%fused_computation.101 | convolution fusion | flops 806092800 | bytes 14942208 | tf_op jit(solution)/shard_map/rqhk,rqhd->rkhd/dot_general | solution.py:199
  269.2 2.3 multiply_reduce_fusion
  271.5 17.0 %fusion.19 = bf16[512,12,1024]{0,2,1:T(8,128)(2,1)} fusion(f32[12,1024,512]{2,1,0:T(8,128)} %get-tuple-element.97, f32[512,12]{0,1:T(8,128)S(1)} %multiply_reduce_fusion, f32[512,12]{0,1:T(8,128)S(1)} %copy-done.36, pred[512,1024]{0,1:T(8,128)(4,1)S(1)} %get-tuple-element.93, bf16[1024,12,64]{0,2,1:T(8,128)(2,1)} %bitcast.338, ...), kind=kOutput, calls=%fused_computation.27 | convolution fusion | flops 855638016 | bytes 40681472 | tf_op jit(solution)/shard_map/rqhd,rkhd->rqhk/dot_general | solution.py:68
  288.5 9.9 %convolution_convert_fusion = bf16[12,64,1024]{2,1,0:T(8,128)(2,1)} fusion(bf16[512,12,64]{0,2,1:T(8,128)(2,1)} %bitcast.328, bf16[512,12,1024]{0,2,1:T(8,128)(2,1)} %fusion.19), kind=kOutput, calls=%fused_computation.100 | convolution fusion | flops 806092800 | bytes 14942208 | tf_op jit(solution)/shard_map/rqhk,rqhd->rkhd/dot_general | solution.py:199
  298.5 2.6 fusion.124
  303.0 5.4 fusion.164
  308.5 5.3 add_convert_fusion.1
  314.5 6.9 %fusion.127 = f32[3072,768]{1,0:T(8,128)S(1)} fusion(bf16[2,512,768]{2,1,0:T(8,128)(2,1)} %param.33, f32[512,3072]{1,0:T(8,128)} %fusion.166, f32[3072]{0:T(1024)S(1)} %copy-done.49), kind=kOutput, calls=%fused_computation.194 | convolution fusion | flops 2431647744 | bytes 16527360 | tf_op jit(solution)/shard_map/rbf,rbd->fd/dot_general | solution.py:161
  321.5 9.2 %add_convert_fusion = bf16[3072,768]{1,0:T(8,128)(2,1)} fusion(f32[3072,768]{1,0:T(8,128)S(1)} %fusion.127, bf16[2,512,768]{2,1,0:T(8,128)(2,1)S(1)} %copy-done.21, f32[512,3072]{1,0:T(8,128)} %copy-done.78, f32[3072]{0:T(1024)S(1)} %copy-done.49), kind=kOutput, calls=%fused_computation.38 | convolution fusion | flops 2436366336 | bytes 21245952 | tf_op jit(solution)/shard_map/rbf,rbd->fd/dot_general | solution.py:161
  333.9 8.4 %convert_reduce_fusion.9 = (f32[12,64]{1,0:T(8,128)S(1)}, bf16[12,64,512]{2,1,0:T(8,128)(2,1)}) fusion(bf16[1024,12,64]{0,2,1:T(8,128)(2,1)} %bitcast.324, bf16[512,12,1024]{0,2,1:T(8,128)(2,1)} %fusion.18), kind=kOutput, calls=%fused_computation.155 | convolution fusion | flops 806485248 | bytes 14945280 | tf_op jit(solution)/shard_map/rqhk,rkhd->rqhd/dot_general | solution.py:196
  342.3 7.9 %convert_reduce_fusion.8 = (f32[12,64]{1,0:T(8,128)S(1)}, bf16[12,64,512]{2,1,0:T(8,128)(2,1)}) fusion(bf16[1024,12,64]{0,2,1:T(8,128)(2,1)S(1)} %bitcast.326, bf16[512,12,1024]{0,2,1:T(8,128)(2,1)} %fusion.19), kind=kOutput, calls=%fused_computation.154 | convolution fusion | flops 806485248 | bytes 14945280 | tf_op jit(solution)/shard_map/rqhk,rkhd->rqhd/dot_general | solution.py:196
  350.3 9.6 %fusion.103 = bf16[1,512,768]{2,1,0:T(8,128)(2,1)} fusion(f32[1,512,768]{2,1,0:T(8,128)} %copy-done.8, bf16[3072,768]{1,0:T(8,128)(2,1)} %param.31, f32[768]{0:T(1024)S(1)} %convert_element_type.480, f32[512,3072]{1,0:T(8,128)} %fusion.166, f32[3072]{0:T(1024)S(1)} %copy-done.49), kind=kOutput, calls=%fused_computation.151 | convolution fusion | flops 2432827392 | bytes 13384704 | tf_op jit(solution)/shard_map/rbf,fd->rbd/dot_general | solution.py:155
  359.8 9.0 %fusion.101 = bf16[1,512,768]{2,1,0:T(8,128)(2,1)} fusion(f32[1,512,768]{2,1,0:T(8,128)S(1)} %copy-done.12, bf16[3072,768]{1,0:T(8,128)(2,1)} %param.31, f32[768]{0:T(1024)S(1)} %convert_element_type.480, f32[512,3072]{1,0:T(8,128)} %copy-done.78, f32[3072]{0:T(1024)S(1)} %copy-done.49), kind=kOutput, calls=%fused_computation.148 | convolution fusion | flops 2432827392 | bytes 13384704 | tf_op jit(solution)/shard_map/rbf,fd->rbd/dot_general | solution.py:155
  368.9 2.0 fusion.176
  371.8 1.9 fusion.177
  374.7 6.7 %fusion.109 = f32[768,1920]{1,0:T(8,128)} fusion(bf16[1,512,384]{1,2,0:T(8,128)(2,1)} %copy.99, bf16[1,512,768]{1,2,0:T(8,128)(2,1)} %reduce-scatter.9.cloned.1.call-done, bf16[1,512,768]{1,2,0:T(8,128)(2,1)} %bitcast.341, f32[768]{0:T(1024)S(1)} %copy-done.60, f32[768]{0:T(1024)S(1)} %copy-done.33, f32[512]{0:T(512)S(1)} %copy-done.53, ...), kind=kOutput, calls=%fused_computation.173 | convolution fusion | flops 1518206976 | bytes 8660992 | tf_op jit(solution)/shard_map/rbd,rbe->de/dot_general | solution.py:224
  381.4 7.2 %add_convert_fusion.2 = bf16[768,1920]{1,0:T(8,128)(2,1)} fusion(f32[768,1920]{1,0:T(8,128)} %fusion.109, bf16[1,512,384]{1,2,0:T(8,128)(2,1)S(1)} %copy-done.29, bf16[1,512,768]{1,2,0:T(8,128)(2,1)} %reduce-scatter.13.cloned.1.call-done, bf16[1,512,768]{1,2,0:T(8,128)(2,1)} %bitcast.343, f32[512]{0:T(512)S(1)} %copy-done.55, f32[512]{0:T(512)S(1)} %copy-done.38, ...), kind=kOutput, calls=%fused_computation.64 | convolution fusion | flops 1521156096 | bytes 11610112 | tf_op jit(solution)/shard_map/rbd,rbe->de/dot_general | solution.py:224
  388.8 2.8 pad_maximum_fusion
  394.0 2.7 fusion.88
  397.9 63.1 %all-reduce.9 = (bf16[768]{0:T(1024)(128)(2,1)S(1)}, bf16[768]{0:T(1024)(128)(2,1)S(1)}, bf16[768]{0:T(1024)(128)(2,1)S(1)}, bf16[384]{0:T(512)(128)(2,1)S(1)}, ...) all-reduce(bf16[768]{0:T(1024)(128)(2,1)S(1)} %add_convert_fusion.1, ...), channel_id=6, replica_groups=mesh['batch'=16,'blk'=2] {'batch'}, use_global_device_ids=true, to_apply=%region_28.29.clone | all-reduce | flops 8832 | bytes 35328
  461.6 5.0 all-reduce.10
  471.3 2.0 pad_maximum_fusion.4
  473.3 72.1 %reduce-scatter.23.cloned.1.call-done = bf16[192,768]{1,0:T(8,128)(2,1)} async-done(((bf16[3072,768]{1,0:T(8,128)(2,1)}), bf16[192,768]{1,0:T(8,128)(2,1)}) %reduce-scatter.23.cloned.1.call-update) | async-done | bytes 294928 | tf_op jit(solution)/shard_map/reduce_scatter | solution.py:255
  545.4 68.0 %reduce-scatter.17.cloned.1.call-done = bf16[48,1920]{1,0:T(8,128)(2,1)} async-done(((bf16[768,1920]{1,0:T(8,128)(2,1)}), bf16[48,1920]{1,0:T(8,128)(2,1)}) %reduce-scatter.17.cloned.1.call-update) | async-done | bytes 184336 | tf_op jit(solution)/shard_map/reduce_scatter | solution.py:255
  613.4 3.9 fusion.87
  618.6 32.6 %all-reduce.14.cloned.1.call-done = (bf16[48,1920]{1,0:T(8,128)(2,1)}, bf16[48,768]{1,0:T(8,128)(2,1)}, bf16[48,3072]{1,0:T(8,128)(2,1)}, bf16[192,768]{1,0:T(8,128)(2,1)}) async-done(((bf16[48,1920]{1,0:T(8,128)(2,1)}, bf16[48,768]{1,0:T(8,128)(2,1)}, bf16[48,3072]{1,0:T(8,128)(2,1)}, bf16[192,768]{1,0:T(8,128)(2,1)}), (bf16[48,1920]{1,0:T(8,128)(2,1)}, bf16[48,768]{1,0:T(8,128)(2,1)}, ...) | async-done | bytes 847888 | tf_op jit(solution)/shard_map/psum | solution.py:257
  (294 shorter events, 46.1 us)
Async XLA Ops:
  7.2 3.9 copy-start
  7.2 39.6 %all-gather.7.cloned.1.call-start = ((), (), s32[]{:S(2)}) async-start(), calls=%async_computation.9 | async-start | bytes 2359296 | tf_op jit(solution)/shard_map/all_gather | solution.py:126
  7.2 3.2 copy-start.2
  9.7 7.5 %copy-start.32 = (f32[768]{0:T(1024)}, f32[768]{0:T(1024)S(1)}, u32[]{:S(2)}) copy-start(f32[768]{0:T(1024)S(1)} %convert_element_type.464) | copy-start | bytes 9220
  10.4 6.8 %copy-start.59 = (f32[768]{0:T(1024)}, f32[768]{0:T(1024)S(1)}, u32[]{:S(2)}) copy-start(f32[768]{0:T(1024)S(1)} %convert_element_type.465) | copy-start | bytes 9220
  10.4 6.8 %copy-start.37 = (f32[512]{0:T(512)}, f32[512]{0:T(512)S(1)}, u32[]{:S(2)}) copy-start(f32[512]{0:T(512)S(1)} %get-tuple-element.120) | copy-start | bytes 6148
  15.9 59.9 %all-gather.5.cloned.1.call-start = ((), (), s32[]{:S(2)}) async-start(), calls=%async_computation.8 | async-start | bytes 2359296 | tf_op jit(solution)/shard_map/all_gather | solution.py:127
  16.0 4.3 copy-start.54
  25.2 4.7 copy-start.47
  25.2 10.2 %copy-start.67 = (bf16[768]{0:T(1024)(128)(2,1)S(1)}, bf16[768]{0:T(1024)(128)(2,1)}, u32[]{:S(2)}) copy-start(bf16[768]{0:T(1024)(128)(2,1)} %param.23) | copy-start | bytes 4612
  25.2 79.0 %all-gather.11.cloned.1.call-start = ((), (), s32[]{:S(2)}) async-start(), calls=%async_computation.11 | async-start | bytes 2359296 | tf_op jit(solution)/shard_map/all_gather | solution.py:126
  27.8 105.4 %all-gather.9.cloned.1.call-start = ((), (), s32[]{:S(2)}) async-start(), calls=%async_computation.10 | async-start | bytes 2359296 | tf_op jit(solution)/shard_map/all_gather | solution.py:127
  29.8 339.0 %reduce-scatter.11.cloned.1.call-start = ((), (), s32[]{:S(2)}) async-start(), calls=%async_computation.13 | async-start | bytes 2359296 | tf_op jit(solution)/shard_map/reduce_scatter | solution.py:210
  35.4 5.7 copy-start.68
  35.4 5.7 copy-start.69
  35.4 5.7 copy-start.70
  35.4 6.3 copy-start.58
  41.1 51.1 %copy-start.63 = (f32[768]{0:T(1024)}, f32[768]{0:T(1024)S(1)}, u32[]{:S(2)}) copy-start(f32[768]{0:T(1024)S(1)} %convert_element_type.474) | copy-start | bytes 9220
  49.4 14.3 %copy-start.15 = (pred[512,1024]{0,1:T(8,128)(4,1)S(1)}, pred[512,1024]{0,1:T(8,128)(4,1)}, u32[]{:S(2)}) copy-start(pred[512,1024]{0,1:T(8,128)(4,1)} %get-tuple-element.92) | copy-start | bytes 1572868
  78.4 13.8 %copy-start.3 = (bf16[2,512,768]{2,1,0:T(8,128)(2,1)S(1)}, bf16[2,512,768]{2,1,0:T(8,128)(2,1)}, u32[]{:S(2)}) copy-start(bf16[2,512,768]{2,1,0:T(8,128)(2,1)} %param.17) | copy-start | bytes 4718596
  78.4 13.8 %copy-start.73 = (bf16[768,768]{1,0:T(8,128)(2,1)S(1)}, bf16[768,768]{1,0:T(8,128)(2,1)}, u32[]{:S(2)}) copy-start(bf16[768,768]{1,0:T(8,128)(2,1)} %param.25) | copy-start | bytes 3538948
  135.8 12.7 %copy-start.4 = (bf16[2,512,768]{2,1,0:T(8,128)(2,1)S(1)}, bf16[2,512,768]{2,1,0:T(8,128)(2,1)}, u32[]{:S(2)}) copy-start(bf16[2,512,768]{2,1,0:T(8,128)(2,1)} %param.17) | copy-start | bytes 4718596
  135.8 12.7 %copy-start.64 = (f32[768]{0:T(1024)S(1)}, f32[768]{0:T(1024)}, u32[]{:S(2)}) copy-start(f32[768]{0:T(1024)} %copy-done.63) | copy-start | bytes 9220
  135.8 12.7 %copy-start.74 = (bf16[768,768]{1,0:T(8,128)(2,1)S(1)}, bf16[768,768]{1,0:T(8,128)(2,1)}, u32[]{:S(2)}) copy-start(bf16[768,768]{1,0:T(8,128)(2,1)} %param.25) | copy-start | bytes 3538948
  148.5 10.0 %slice-start = ((s8[4718592]{0:T(1024)(128)(4,1)}), s8[4194304]{0:T(1024)(128)(4,1)S(1)}, s32[]{:S(2)}) async-start(s8[4718592]{0:T(1024)(128)(4,1)} %bitcast.359), calls=%async_computation.21 | async-start | bytes 8388608
  149.4 39.9 %copy-start.10 = (f32[1,512,768]{2,1,0:T(8,128)}, f32[1,512,768]{2,1,0:T(8,128)S(1)}, u32[]{:S(2)}) copy-start(f32[1,512,768]{2,1,0:T(8,128)S(1)} %get-tuple-element.101) | copy-start | bytes 4718596
  150.1 39.2 %copy-start.56 = (f32[512]{0:T(512)}, f32[512]{0:T(512)S(1)}, u32[]{:S(2)}) copy-start(f32[512]{0:T(512)S(1)} %add_rsqrt_fusion) | copy-start | bytes 6148
  150.1 8.3 %slice-start.1 = ((s8[4718592]{0:T(1024)(128)(4,1)}), s8[524288]{0:T(1024)(128)(4,1)S(1)}, s32[]{:S(2)}) async-start(s8[4718592]{0:T(1024)(128)(4,1)} %bitcast.359), calls=%async_computation.22 | async-start | bytes 1048576
  150.1 11.1 %slice-start.2 = ((s8[4718592]{0:T(1024)(128)(4,1)}), s8[4194304]{0:T(1024)(128)(4,1)S(1)}, s32[]{:S(2)}) async-start(s8[4718592]{0:T(1024)(128)(4,1)} %bitcast.361), calls=%async_computation.23 | async-start | bytes 8388608
  161.3 12.3 %copy-start.78 = (f32[512,3072]{1,0:T(8,128)}, f32[512,3072]{1,0:T(8,128)S(1)}, u32[]{:S(2)}) copy-start(f32[512,3072]{1,0:T(8,128)S(1)} %fusion.162) | copy-start | bytes 18874372
  213.1 158.7 %reduce-scatter.15.cloned.1.call-start = ((), (), s32[]{:S(2)}) async-start(), calls=%async_computation.15 | async-start | bytes 2359296 | tf_op jit(solution)/shard_map/reduce_scatter | solution.py:210
  224.3 12.9 %copy-start.35 = (f32[512,12]{0,1:T(8,128)}, f32[512,12]{0,1:T(8,128)S(1)}, u32[]{:S(2)}) copy-start(f32[512,12]{0,1:T(8,128)S(1)} %log_add_fusion) | copy-start | bytes 73732
  242.1 132.6 %reduce-scatter.9.cloned.1.call-start = ((), (), s32[]{:S(2)}) async-start(), calls=%async_computation.12 | async-start | bytes 2359296 | tf_op jit(solution)/shard_map/reduce_scatter | solution.py:207
  269.1 112.3 %reduce-scatter.13.cloned.1.call-start = ((), (), s32[]{:S(2)}) async-start(), calls=%async_computation.14 | async-start | bytes 2359296 | tf_op jit(solution)/shard_map/reduce_scatter | solution.py:207
  298.4 174.9 %reduce-scatter.19.cloned.1.call-start = ((), (), s32[]{:S(2)}) async-start(), calls=%async_computation.17 | async-start | bytes 1253376 | tf_op jit(solution)/shard_map/reduce_scatter | solution.py:255
  302.9 5.5 copy-start.57
  303.0 170.4 %reduce-scatter.21.cloned.1.call-start = ((), (), s32[]{:S(2)}) async-start(), calls=%async_computation.18 | async-start | bytes 5013504 | tf_op jit(solution)/shard_map/reduce_scatter | solution.py:255
  303.0 5.4 copy-start.11
  303.0 5.4 copy-start.81
  313.8 231.6 %reduce-scatter.23.cloned.1.call-start = ((), (), s32[]{:S(2)}) async-start(), calls=%async_computation.19 | async-start | bytes 5013504 | tf_op jit(solution)/shard_map/reduce_scatter | solution.py:255
  314.5 6.9 %copy-start.21 = (bf16[2,512,768]{2,1,0:T(8,128)(2,1)S(1)}, bf16[2,512,768]{2,1,0:T(8,128)(2,1)}, u32[]{:S(2)}) copy-start(bf16[2,512,768]{2,1,0:T(8,128)(2,1)} %param.33) | copy-start | bytes 4718596
  330.7 3.2 copy-start.71
  330.7 282.7 %reduce-scatter.17.cloned.1.call-start = ((), (), s32[]{:S(2)}) async-start(), calls=%async_computation.16 | async-start | bytes 3133440 | tf_op jit(solution)/shard_map/reduce_scatter | solution.py:255
  333.9 8.4 %copy-start.1 = (bf16[1,1024,768]{1,2,0:T(8,128)(2,1)S(1)}, bf16[1,1024,768]{1,2,0:T(8,128)(2,1)}, u32[]{:S(2)}) copy-start(bf16[1,1024,768]{1,2,0:T(8,128)(2,1)} %copy.90) | copy-start | bytes 4718596
  350.3 9.6 %copy-start.12 = (f32[1,512,768]{2,1,0:T(8,128)S(1)}, f32[1,512,768]{2,1,0:T(8,128)}, u32[]{:S(2)}) copy-start(f32[1,512,768]{2,1,0:T(8,128)} %copy-done.10) | copy-start | bytes 4718596
  368.9 5.8 copy-start.33
  368.9 5.8 copy-start.40
  368.9 5.8 copy-start.53
  368.9 5.8 copy-start.60
  374.7 6.7 %copy-start.29 = (bf16[1,512,384]{1,2,0:T(8,128)(2,1)S(1)}, bf16[1,512,384]{1,2,0:T(8,128)(2,1)}, u32[]{:S(2)}) copy-start(bf16[1,512,384]{1,2,0:T(8,128)(2,1)} %copy.106) | copy-start | bytes 1179652
  374.7 6.7 %copy-start.38 = (f32[512]{0:T(512)S(1)}, f32[512]{0:T(512)}, u32[]{:S(2)}) copy-start(f32[512]{0:T(512)} %copy-done.37) | copy-start | bytes 6148
  374.7 6.7 %copy-start.55 = (f32[512]{0:T(512)S(1)}, f32[512]{0:T(512)}, u32[]{:S(2)}) copy-start(f32[512]{0:T(512)} %copy-done.54) | copy-start | bytes 6148
  388.7 3.0 copy-start.65
  388.7 3.0 copy-start.66
  388.7 3.0 copy-start.41
  388.7 3.0 copy-start.42
  388.7 3.1 copy-start.50
  388.7 3.1 copy-start.51
  388.8 262.4 %all-reduce.14.cloned.1.call-start = ((), (), s32[]{:S(2)}) async-start(), calls=%async_computation.20 | async-start | bytes 1695744 | tf_op jit(solution)/shard_map/psum | solution.py:257
  388.8 3.1 copy-start.19
  388.8 3.2 copy-start.24
  388.8 3.2 copy-start.76
  396.7 74.6 %copy-start.22 = (bf16[1,512,384]{2,1,0:T(8,128)(2,1)S(1)}, bf16[1,512,384]{2,1,0:T(8,128)(2,1)}, u32[]{:S(2)}) copy-start(bf16[1,512,384]{2,1,0:T(8,128)(2,1)} %get-tuple-element.74) | copy-start | bytes 1179652
  651.2 5.4 copy-start.31
  (35 other events, 71.4 us)
Sparse Core Ops, SparseCore 0:
  16.0 29.9 all-gather.6
  47.6 27.2 all-gather.4
  77.0 27.2 all-gather.10
  105.6 27.1 all-gather.8
  213.2 26.3 reduce-scatter.10
  242.2 26.2 reduce-scatter.14
  270.7 26.0 reduce-scatter.8
  299.7 26.0 reduce-scatter.12
  329.5 58.0 reduce-scatter.18
  391.3 74.9 reduce-scatter.20
  470.7 74.6 reduce-scatter.22
  549.1 64.2 reduce-scatter.16
  615.9 35.2 all-reduce.13
where the time goes:
time: 669 us; the launch traced here: 664 us
  matrix products  269 us (40%)
  waiting for transfers between devices  182 us (27%)
  blocking collectives  73.5 us (11%)
  other arithmetic  69.6 us (10%)
  local copies, waits for them, and re-layouts  51.7 us (8%)
  between operations  17.3 us (3%)
    reduce_scatter x4, waiting for transfers between devices, local(): lax.psum_scatter(as_sent(totals), 'batch', scatter_dimension=0, tiled=True)  140 us
    unnamed x1, blocking collectives  63.1 us
    dot_general x2, matrix products, grad_block(): jnp.einsum('rqhd,rkhd->rqhk', dout4, value4, preferred_element_type=jnp.f...  34 us
    psum x1, waiting for transfers between devices, local(): lax.psum(as_sent(totals), 'blk')  32.6 us
    dot_general x2, matrix products, score_block(): jnp.einsum('rqhd,rkhd->rqhk', query4, key4, preferred_element_type=jnp.fl...  28.4 us
    dot_general x2, matrix products, local(): jnp.einsum('rqhk,rkhd->rqhd', weights.astype(jnp.bfloat16), heads_of(valu...  26.5 us
    dot_general x2, matrix products, local(): jnp.einsum('rqhk,rqhd->rkhd', probs_low, dout4, preferred_element_type=jn...  25.6 us
    reduce_sum x2, other arithmetic, local(): new_sum = jnp.sum(weights, axis=-1)  22.9 us
  transfers between devices with their start and end apart: 13, of which 4 were waited for; matrix products, arithmetic and copies ran while one was open for 44% of the time, Pallas kernels for 0%

commit v1 on v0

--- a/solution.py
+++ b/solution.py
@@ -1,15 +1,597 @@
+import functools
+
 import jax
 import jax.numpy as jnp
 from jax import lax
+from jax.experimental import pallas as pl
+from jax.experimental.pallas import tpu as pltpu
 from jax.sharding import PartitionSpec as P
 
 HEADS = 12
 HEAD_DIM = 64
-MICRO = 2
-
-
+PAIRS = HEADS // 2
+LANES = 2 * HEAD_DIM
 EPS = 1e-05
 NEG = -1e30
+QB = 256
+F32 = jnp.float32
+BF = jnp.bfloat16
+MIB = 2**20
+MESH = pl.DeviceIdType.MESH
+
+
+def nn(a, b):
+    return lax.dot_general(a, b, (((1,), (0,)), ((), ())), preferred_element_type=F32)
+
+
+def nt(a, b):
+    return lax.dot_general(a, b, (((1,), (1,)), ((), ())), preferred_element_type=F32)
+
+
+def tn(a, b):
+    return lax.dot_general(a, b, (((0,), (0,)), ((), ())), preferred_element_type=F32)
+
+
+def norm_parts(rows):
+    mean = jnp.mean(rows, axis=-1, keepdims=True)
+    centred = rows - mean
+    inverse = lax.rsqrt(jnp.mean(centred * centred, axis=-1, keepdims=True) + EPS)
+    return centred * inverse, inverse
+
+
+def norm_pull(grad, xhat, inverse, gain):
+    scaled = grad * gain
+    first = jnp.mean(scaled, axis=-1, keepdims=True)
+    second = jnp.mean(scaled * xhat, axis=-1, keepdims=True)
+    return inverse * (scaled - first - xhat * second)
+
+
+def column_sum(rows):
+    return jnp.sum(rows, axis=0, keepdims=True)
+
+
+def front_kernel(
+    x_in,
+    fv_in,
+    seg_in,
+    cot_in,
+    g1_ref,
+    b1_ref,
+    wqkv_in,
+    bq_ref,
+    bv_ref,
+    wout_in,
+    bout_ref,
+    g2_ref,
+    b2_ref,
+    x_out,
+    q_out,
+    k_out,
+    v_out,
+    att_out,
+    act2_out,
+    mid_out,
+    lse_ref,
+    bias_out,
+    cot_out,
+    xs,
+    qs,
+    ks,
+    vs,
+    atts,
+    act2s,
+    mids,
+    bias,
+    wqkv,
+    wout,
+    segrow,
+    segsend,
+    segcol,
+    in_sem,
+    out_sem,
+    send_sem,
+    recv_sem,
+):
+    half = x_in.shape[1]
+    tokens = 2 * half
+    width = x_in.shape[2]
+    val = fv_in.shape[2]
+    steps = tokens // QB
+    me = lax.axis_index("blk")
+    other = 1 - me
+    mine = pl.multiple_of(me * half, half)
+    theirs = pl.multiple_of(other * half, half)
+
+    def local_in(i, src, dst):
+        copy = pltpu.make_async_copy(src, dst, in_sem.at[i])
+        copy.start()
+        return copy
+
+    own_x = local_in(0, x_in.at[me], xs.at[pl.ds(mine, half)])
+    own_fv = local_in(1, fv_in.at[me], vs.at[pl.ds(mine, half), pl.ds(val, val)])
+    own_w = local_in(2, wqkv_in, wqkv)
+    own_wo = local_in(3, wout_in, wout)
+    own_cot = local_in(4, cot_in.at[me], cot_out.at[pl.ds(mine, half)])
+    first, second = seg_in[0:1, :], seg_in[1:2, :]
+    segsend[...] = jnp.broadcast_to(jnp.where(me == 0, second, first), segsend.shape)
+
+    barrier = pltpu.get_barrier_semaphore()
+    pl.semaphore_signal(barrier, inc=1, device_id={"blk": other}, device_id_type=MESH)
+    pl.semaphore_wait(barrier, 1)
+
+    def remote(i, src, dst):
+        copy = pltpu.make_async_remote_copy(
+            src_ref=src,
+            dst_ref=dst,
+            send_sem=send_sem.at[i],
+            recv_sem=recv_sem.at[i],
+            device_id={"blk": other},
+            device_id_type=MESH,
+        )
+        copy.start()
+        return copy
+
+    part = half // 2
+    far_x = [
+        remote(
+            c,
+            x_in.at[other, pl.ds(c * part, part)],
+            xs.at[pl.ds(pl.multiple_of(mine + c * part, part), part)],
+        )
+        for c in range(2)
+    ]
+    far_seg = remote(2, segsend, segrow.at[:, pl.ds(mine, half)])
+    far_fv = remote(3, fv_in.at[other], vs.at[pl.ds(mine, half), pl.ds(val, val)])
+    far_cot = remote(4, cot_in.at[other], cot_out.at[pl.ds(mine, half)])
+
+    own_row = jnp.broadcast_to(jnp.where(me == 0, first, second), (8, half))
+    segrow[:, pl.ds(mine, half)] = own_row
+
+    def project(start):
+        rows = pl.ds(pl.multiple_of(start, QB), QB)
+        xhat, _ = norm_parts(xs[rows, :].astype(F32))
+        act1 = (xhat * g1_ref[...].astype(F32) + b1_ref[...].astype(F32)).astype(BF)
+        out = nn(act1, wqkv[...])
+        query = (out[:, :width] + bq_ref[...].astype(F32)).astype(BF)
+        qs[rows, :] = query * jnp.asarray(HEAD_DIM**-0.5, BF)
+        ks[rows, :] = out[:, width : 2 * width].astype(BF)
+        vs[rows, pl.ds(0, val)] = (out[:, 2 * width :] + bv_ref[...].astype(F32)).astype(BF)
+
+    own_x.wait()
+    own_w.wait()
+    for c in range(2):
+        project(mine + c * QB)
+    for c in range(2):
+        far_x[c].wait()
+        project(theirs + c * part)
+
+    outs = []
+
+    def local_out(src, dst):
+        copy = pltpu.make_async_copy(src, dst, out_sem.at[len(outs)])
+        copy.start()
+        outs.append(copy)
+
+    local_out(xs, x_out)
+    local_out(qs, q_out)
+    local_out(ks, k_out)
+
+    far_seg.wait()
+    for c in range(tokens // LANES):
+        row = segrow[0:1, c * LANES : (c + 1) * LANES].astype(F32)
+        segcol[c * LANES : (c + 1) * LANES, :] = jnp.broadcast_to(row, (LANES, LANES)).T
+    for j in range(steps):
+        key = segcol[j * QB : (j + 1) * QB, :]
+        key = jnp.concatenate([key] * (QB // LANES), axis=1)
+        for i in range(j, steps):
+            query = segrow[0:1, i * QB : (i + 1) * QB].astype(F32)
+            seen = (key == query) & (query >= 0.0)
+            if i == j:
+                down = lax.broadcasted_iota(jnp.int32, (QB, QB), 0)
+                across = lax.broadcasted_iota(jnp.int32, (QB, QB), 1)
+                seen = (seen & (down <= across)) | (down == across)
+            bias[j * QB : (j + 1) * QB, i * QB : (i + 1) * QB] = jnp.where(seen, 0.0, NEG)
+        cut = (pl.ds(j * QB, QB), pl.ds(j * QB, tokens - j * QB))
+        local_out(bias.at[cut], bias_out.at[cut])
+    own_fv.wait()
+    far_fv.wait()
+    local_out(vs, v_out)
+
+    low = lax.broadcasted_iota(jnp.int32, (1, LANES), 1) < HEAD_DIM
+
+    @pl.loop(0, PAIRS)
+    def _(p):
+        cols = pl.ds(pl.multiple_of(p * LANES, LANES), LANES)
+        k = ks[:, cols]
+        v = vs[:, cols]
+
+        def score(i, h):
+            q = qs[i * QB : (i + 1) * QB, cols]
+            q = jnp.where(low if h == 0 else ~low, q, jnp.zeros_like(q))
+            span = (i + 1) * QB
+            return nt(k[:span], q) + bias[:span, i * QB : span]
+
+        done = {}
+
+        def finish(i, h, s):
+            span = (i + 1) * QB
+            top = jnp.max(s, axis=0, keepdims=True)
+            e = jnp.exp(s - top)
+            total = jnp.sum(e, axis=0, keepdims=True)
+            done[h] = tn((e * (1.0 / total)).astype(BF), v[:span])
+            lse_ref[p, h : h + 1, i * QB : span] = top + jnp.log(total)
+            if h == 1:
+                atts[i * QB : span, cols] = jnp.where(low, done[0], done[1]).astype(BF)
+
+        waiting = []
+        for i in range(steps):
+            for h in range(2):
+                waiting.append((i, h, score(i, h)))
+                if len(waiting) > 2:
+                    finish(*waiting.pop(0))
+        for item in waiting:
+            finish(*item)
+
+    local_out(atts, att_out)
+    own_wo.wait()
+    for c in range(steps):
+        rows = slice(c * QB, (c + 1) * QB)
+        middle = xs[rows, :].astype(F32) + nn(atts[rows, :], wout[...]) + bout_ref[...].astype(F32)
+        mids[rows, :] = middle
+        xhat, _ = norm_parts(middle)
+        act2s[rows, :] = (xhat * g2_ref[...].astype(F32) + b2_ref[...].astype(F32)).astype(BF)
+    local_out(mids, mid_out)
+    local_out(act2s, act2_out)
+    for copy in outs:
+        copy.wait()
+    own_cot.wait()
+    far_cot.wait()
+
+
+def front(x, fv, seg, cot, g1, b1, wqkv, bq, bv, wout, bout, g2, b2):
+    half, width, val = x.shape[1], x.shape[2], fv.shape[2]
+    tokens = 2 * half
+    hbm = pl.BlockSpec(memory_space=pl.ANY)
+    vmem = pl.BlockSpec(memory_space=pltpu.VMEM)
+    flat = jax.ShapeDtypeStruct((tokens, width), BF)
+    shape = jax.ShapeDtypeStruct
+    return pl.pallas_call(
+        front_kernel,
+        in_specs=[hbm, hbm, vmem, hbm, vmem, vmem, hbm, vmem, vmem, hbm, vmem, vmem, vmem],
+        out_specs=[hbm] * 7 + [vmem] + [hbm] * 2,
+        out_shape=[
+            flat,
+            flat,
+            flat,
+            flat,
+            flat,
+            flat,
+            shape((tokens, width), F32),
+            shape((PAIRS, 2, tokens), F32),
+            shape((tokens, tokens), F32),
+            flat,
+        ],
+        scratch_shapes=[
+            pltpu.VMEM((tokens, width), BF),
+            pltpu.VMEM((tokens, width), BF),
+            pltpu.VMEM((tokens, width), BF),
+            pltpu.VMEM((tokens, width), BF),
+            pltpu.VMEM((tokens, width), BF),
+            pltpu.VMEM((tokens, width), BF),
+            pltpu.VMEM((tokens, width), F32),
+            pltpu.VMEM((tokens, tokens), F32),
+            pltpu.VMEM(wqkv.shape, BF),
+            pltpu.VMEM(wout.shape, BF),
+            pltpu.VMEM((8, tokens), jnp.int32),
+            pltpu.VMEM((8, half), jnp.int32),
+            pltpu.VMEM((tokens, LANES), F32),
+            pltpu.SemaphoreType.DMA((5,)),
+            pltpu.SemaphoreType.DMA((7 + tokens // QB,)),
+            pltpu.SemaphoreType.DMA((5,)),
+            pltpu.SemaphoreType.DMA((5,)),
+        ],
+        compiler_params=pltpu.CompilerParams(
+            collective_id=0, has_side_effects=True, vmem_limit_bytes=56 * MIB
+        ),
+        name="front",
+    )(x, fv, seg, cot, g1, b1, wqkv, bq, bv, wout, bout, g2, b2)
+
+
+def feed_kernel(
+    act2,
+    cot,
+    mid,
+    att,
+    g2_ref,
+    bproj_ref,
+    wout,
+    wfc,
+    bfc_ref,
+    wproj,
+    lout,
+    gmid,
+    gatt,
+    dots,
+    dwout,
+    dwfc,
+    dwproj,
+    dbfc,
+    small,
+    acc,
+    dact,
+    act2t,
+    hid,
+    dpre,
+    sel,
+):
+    t = pl.program_id(0)
+    tokens, width = act2.shape
+    steps = tokens // QB
+
+    @pl.when(t == 0)
+    def _():
+        act2t[...] = act2[...].T
+        acc[...] = jnp.zeros_like(acc)
+        dact[...] = jnp.zeros_like(dact)
+        head = lax.broadcasted_iota(jnp.int32, sel.shape, 0)
+        feature = lax.broadcasted_iota(jnp.int32, sel.shape, 1)
+        inside = (feature >= head * HEAD_DIM) & (feature < (head + 1) * HEAD_DIM)
+        sel[...] = jnp.where(inside, 1.0, 0.0).astype(BF)
+
+    total = None
+    for c in range(steps):
+        rows = slice(c * QB, (c + 1) * QB)
+        u = nn(act2[rows, :], wfc[...]) + bfc_ref[...].astype(F32)
+        square = u * u
+        bend = jnp.tanh(u * (0.7978845608028654 + (0.7978845608028654 * 0.044715) * square))
+        halfway = 0.5 + 0.5 * bend
+        hidden = (u * halfway).astype(BF)
+        hid[rows, :] = hidden
+        acc[rows, :] += nn(hidden, wproj[...])
+        slope = halfway + (u * (0.5 - 0.5 * bend * bend)) * (
+            0.7978845608028654 + (3 * 0.7978845608028654 * 0.044715) * square
+        )
+        grad = (nt(cot[rows, :], wproj[...]) * slope).astype(BF)
+        dpre[rows, :] = grad
+        dact[rows, :] += nt(grad, wfc[...])
+        part = column_sum(grad.astype(F32))
+        total = part if total is None else total + part
+    dbfc[...] = total
+    dwproj[...] = tn(hid[...], cot[...]).astype(BF)
+    dwfc[...] = nn(act2t[...], dpre[...]).astype(BF)
+
+    @pl.when(t == pl.num_programs(0) - 1)
+    def _():
+        gain = g2_ref[...].astype(F32)
+        sums = [None] * 4
+        for c in range(steps):
+            rows = slice(c * QB, (c + 1) * QB)
+            middle = mid[rows, :]
+            upstream = cot[rows, :].astype(F32)
+            lout[rows, :] = (middle + acc[rows, :] + bproj_ref[...].astype(F32)).astype(BF)
+            xhat, inverse = norm_parts(middle)
+            da = dact[rows, :]
+            grad_middle = upstream + norm_pull(da, xhat, inverse, gain)
+            gmid[rows, :] = grad_middle
+            branch = grad_middle.astype(BF)
+            hid[rows, :width] = branch
+            parts = [
+                column_sum(upstream),
+                column_sum(da * xhat),
+                column_sum(da),
+                column_sum(branch.astype(F32)),
+            ]
+            sums = [b if a is None else a + b for a, b in zip(sums, parts)]
+            ga = nt(branch, wout[...]).astype(BF)
+            gatt[rows, :] = ga
+            product = ga.astype(F32) * att[rows, :].astype(F32)
+            big = product.astype(BF)
+            rest = (product - big.astype(F32)).astype(BF)
+            both = nt(sel[...], big) + nt(sel[...], rest)
+            for p in range(PAIRS):
+                dots[p, :, rows] = both[2 * p : 2 * p + 2, :]
+        small[...] = jnp.concatenate(sums + [jnp.zeros((4, width), F32)], axis=0)
+        dwout[...] = tn(att[...], hid[:, :width]).astype(BF)
+
+
+def feed(act2, cot, mid, att, g2, bproj, wout, wfc, bfc, wproj):
+    tokens, width = act2.shape
+    ff = wfc.shape[1]
+    tile = 768
+    shape = jax.ShapeDtypeStruct
+    flat = shape((tokens, width), BF)
+
+    def whole(s):
+        return pl.BlockSpec(s, lambda t: (0,) * len(s))
+
+    rows = whole((tokens, width))
+    line = whole((1, width))
+    return pl.pallas_call(
+        feed_kernel,
+        grid=(ff // tile,),
+        in_specs=[
+            rows,
+            rows,
+            rows,
+            rows,
+            line,
+            line,
+            whole(wout.shape),
+            pl.BlockSpec((width, tile), lambda t: (0, t)),
+            pl.BlockSpec((1, tile), lambda t: (0, t)),
+            pl.BlockSpec((tile, width), lambda t: (t, 0)),
+        ],
+        out_specs=[
+            rows,
+            rows,
+            rows,
+            whole((PAIRS, 2, tokens)),
+            whole(wout.shape),
+            pl.BlockSpec((width, tile), lambda t: (0, t)),
+            pl.BlockSpec((tile, width), lambda t: (t, 0)),
+            pl.BlockSpec((1, tile), lambda t: (0, t)),
+            whole((8, width)),
+        ],
+        out_shape=[
+            flat,
+            shape((tokens, width), F32),
+            flat,
+            shape((PAIRS, 2, tokens), F32),
+            shape(wout.shape, BF),
+            shape(wfc.shape, BF),
+            shape(wproj.shape, BF),
+            shape((1, ff), F32),
+            shape((8, width), F32),
+        ],
+        scratch_shapes=[
+            pltpu.VMEM((tokens, width), F32),
+            pltpu.VMEM((tokens, width), F32),
+            pltpu.VMEM((width, tokens), BF),
+            pltpu.VMEM((tokens, tile), BF),
+            pltpu.VMEM((tokens, tile), BF),
+            pltpu.VMEM((16, width), BF),
+        ],
+        compiler_params=pltpu.CompilerParams(vmem_limit_bytes=60 * MIB),
+        name="feed",
+    )(act2, cot, mid, att, g2, bproj, wout, wfc, bfc, wproj)
+
+
+def back_kernel(q_ref, k_ref, v_ref, do_ref, lse_ref, d_ref, bias, dq_ref, dk_ref, dv_ref, dqa):
+    tokens = q_ref.shape[0]
+    steps = tokens // QB
+    low = lax.broadcasted_iota(jnp.int32, (1, LANES), 1) < HEAD_DIM
+    masks = [low, ~low]
+    zero = jnp.zeros((), BF)
+    q, k, v, do = q_ref[...], k_ref[...], v_ref[...], do_ref[...]
+    qm = [jnp.where(m, q, zero) for m in masks]
+    km = [jnp.where(m, k, zero) for m in masks]
+    dom = [jnp.where(m, do, zero) for m in masks]
+    for j in range(steps):
+        a = j * QB
+        keys = slice(a, a + QB)
+        dk = dv = dq = None
+        for h in range(2):
+            s = nt(k[keys], qm[h][a:]) + bias[keys, a:]
+            probs = jnp.exp(s - lse_ref[0, h : h + 1, a:])
+            dp = nt(v[keys], dom[h][a:])
+            ds = (probs * (dp - d_ref[0, h : h + 1, a:])).astype(BF)
+            dvh = nn(probs.astype(BF), dom[h][a:])
+            dkh = nn(ds, qm[h][a:])
+            dqh = tn(ds, km[h][keys])
+            dk = dkh if dk is None else dk + dkh
+            dv = dvh if dv is None else dv + dvh
+            dq = dqh if dq is None else dq + dqh
+        dk_ref[keys, :] = dk.astype(BF)
+        dv_ref[keys, :] = dv.astype(BF)
+        if j == 0:
+            dqa[...] = dq
+        else:
+            dqa[a:, :] += dq
+    dq_ref[...] = (dqa[...] * HEAD_DIM**-0.5).astype(BF)
+
+
+def back(q, k, v, do, lse, dots, bias):
+    tokens, width = q.shape
+    pair = pl.BlockSpec((tokens, LANES), lambda p: (0, p))
+    stat = pl.BlockSpec((1, 2, tokens), lambda p: (p, 0, 0))
+    flat = jax.ShapeDtypeStruct((tokens, width), BF)
+    return pl.pallas_call(
+        back_kernel,
+        grid=(PAIRS,),
+        in_specs=[pair] * 4
+        + [stat, stat, pl.BlockSpec((tokens, tokens), lambda p: (0, 0))],
+        out_specs=[pair] * 3,
+        out_shape=[flat] * 3,
+        scratch_shapes=[pltpu.VMEM((tokens, LANES), F32)],
+        compiler_params=pltpu.CompilerParams(vmem_limit_bytes=60 * MIB),
+        name="back",
+    )(q, k, v, do, lse, dots, bias)
+
+
+def swap_back(rows, half):
+    me = lax.axis_index("blk")
+    own = lax.dynamic_slice_in_dim(rows, me * half, half, 0)
+    give = lax.dynamic_slice_in_dim(rows, (1 - me) * half, half, 0)
+    got = lax.ppermute(give, "blk", [(0, 1), (1, 0)])
+    return jnp.stack([jnp.where(me == 0, own, got), jnp.where(me == 0, got, own)])
+
+
+def paired(
+    inputs,
+    first_values,
+    segments,
+    ln1_gain,
+    first_norm_bias,
+    w_qkv,
+    b_query,
+    b_value,
+    w_out,
+    b_out,
+    ln2_gain,
+    second_norm_bias,
+    w_fc,
+    b_fc,
+    w_proj,
+    b_proj,
+    cotangent,
+):
+    half, width = inputs.shape[1], inputs.shape[2]
+    val = first_values.shape[2]
+    line = lambda a: a.reshape(1, -1)
+    x, q, k, v, att, act2, mid, lse, bias, cot = front(
+        inputs,
+        first_values,
+        segments,
+        cotangent,
+        line(ln1_gain),
+        line(first_norm_bias),
+        w_qkv,
+        line(b_query),
+        line(b_value),
+        w_out,
+        line(b_out),
+        line(ln2_gain),
+        line(second_norm_bias),
+    )
+    lout, gmid, gatt, dots, dwout, dwfc, dwproj, dbfc, small = feed(
+        act2, cot, mid, att, line(ln2_gain), line(b_proj), w_out, w_fc, line(b_fc), w_proj
+    )
+    dq, dk, dv = back(q, k, v, gatt, lse, dots, bias)
+    gain = ln1_gain.astype(F32)
+    xhat, inverse = norm_parts(x.astype(F32))
+    act1 = (xhat * gain + first_norm_bias.astype(F32)).astype(BF)
+    gqkv = jnp.concatenate([dq, dk, dv[:, :val]], axis=1)
+    dwqkv = tn(act1, gqkv).astype(BF)
+    da = nt(gqkv, w_qkv)
+    gx = (gmid + norm_pull(da, xhat, inverse, gain)).astype(BF)
+    gathered = (
+        jnp.sum(da * xhat, axis=0),
+        jnp.sum(da, axis=0),
+        dwqkv,
+        jnp.sum(dq.astype(F32), axis=0),
+        jnp.sum(dv[:, :val].astype(F32), axis=0),
+        dwout,
+        small[3],
+        small[1],
+        small[2],
+        dwfc,
+        dbfc[0],
+        dwproj,
+        small[0],
+    )
+    totals = tuple(
+        lax.psum_scatter(part.astype(BF), "batch", scatter_dimension=0, tiled=True)
+        for part in gathered
+    )
+    totals = tuple(part.astype(F32) for part in lax.psum(totals, "blk"))
+    return (
+        swap_back(lout, half),
+        swap_back(gx, half),
+        swap_back(dv[:, val:], half),
+    ) + totals
+
+
+MICRO = 2
 
 
 def as_sent(shard):
@@ -72,7 +654,7 @@
     return (probs_low, grad_scores)
 
 
-def local(
+def spread(
     inputs,
     first_values,
     segments,
@@ -262,47 +844,20 @@
     ) + tuple(totals)
 
 
+def layer(inputs, *rest):
+    whole_rows = lax.axis_size("blk") == inputs.shape[0] == 2 and inputs.shape[1] == 2 * QB
+    return (paired if whole_rows else spread)(inputs, *rest)
+
+
 def solution(mesh):
-    placed = (
-        P("batch", "blk", None),
-        P("batch", "blk", None),
-        P("batch", "blk"),
-        P(),
-        P(),
-        P(),
-        P(),
-        P(),
-        P(),
-        P(),
-        P(),
-        P(),
-        P(),
-        P(),
-        P(),
-        P(),
-        P("batch", "blk", None),
-    )
+    rows = P("batch", "blk", None)
+    flat = P("batch")
+    wide = P("batch", None)
     return jax.shard_map(
-        local,
+        layer,
         mesh=mesh,
-        in_specs=placed,
-        out_specs=(
-            P("batch", "blk", None),
-            P("batch", "blk", None),
-            P("batch", "blk", None),
-            P("batch"),
-            P("batch"),
-            P("batch", None),
-            P("batch"),
-            P("batch"),
-            P("batch", None),
-            P("batch"),
-            P("batch"),
-            P("batch"),
-            P("batch", None),
-            P("batch"),
-            P("batch", None),
-            P("batch"),
-        ),
+        in_specs=(rows, rows, P("batch", "blk")) + (P(),) * 13 + (rows,),
+        out_specs=(rows, rows, rows)
+        + (flat, flat, wide, flat, flat, wide, flat, flat, flat, wide, flat, wide, flat),
         check_vma=False,
     )

time: 669 us -> 463 us (0.69)
  matrix products: 269 us -> 13 us
  Pallas kernels: 0 us -> 128 us
  other arithmetic: 69.6 us -> 33.3 us
  local copies, waits for them, and re-layouts: 51.7 us -> 24 us
  waiting for transfers between devices: 182 us -> 172 us
  blocking collectives: 73.5 us -> 64.7 us
    dot_general x36 -> x2, matrix products: 269 us -> 13 us  [the longest x1 7.57 us: nt(): lax.dot_general(a, b, (((1,), (1,)), ((), ())), preferred_element_type=F32)]
    pallas_call x0 -> x3, Pallas kernels: none -> 128 us  [the longest x1 51.1 us: front(): pl.pallas_call(front_kernel, in_specs=[hbm, hbm, vmem, hbm, vmem, vmem, h...]
    reduce_sum x13 -> x4, other arithmetic: 35.2 us -> 5.79 us  [the longest x1 3.21 us: paired(): jnp.sum(dv[:, :val].astype(F32), axis=0)]
    convert_element_type x9 -> x0, local copies, waits for them, and re-layouts: 19.9 us -> none  [the longest x2 5.41 us: local(): out_dot = jnp.sum(dout4.astype(jnp.float32) * attention4, axis=-1)]
    reshape x0 -> x9, local copies, waits for them, and re-layouts: none -> 11.4 us  [paired(): line = lambda a: a.reshape(1, -1)]
    all_gather x4 -> x0, local copies, waits for them, and re-layouts: 10.6 us -> none  [the longest x2 5.38 us: local(): key_part = lax.all_gather(keys_low, 'blk', axis=1, tiled=True)]
    slice x9 -> x1, local copies, waits for them, and re-layouts: 10.5 us -> 0.63 us  [paired(): small[0]]
    all_gather x4 -> x0, waiting for transfers between devices: 9.55 us -> none  [the longest x2 9.53 us: local(): key_part = lax.all_gather(keys_low, 'blk', axis=1, tiled=True)]
  transfers between devices with their start and end apart: 13 -> 8, of which waited for: 4 -> 3; matrix products, arithmetic and copies ran while one was open for 44% -> 11% of each run, Pallas kernels for 0% -> 6%
where the time goes in v1:
time: 463 us; the launch traced here: 456 us
  waiting for transfers between devices  172 us (37%)
  Pallas kernels  128 us (28%)
  blocking collectives  64.7 us (14%)
  other arithmetic  33.3 us (7%)
  local copies, waits for them, and re-layouts  24 us (5%)
  between operations  16.4 us (4%)
  matrix products  13 us (3%)
    reduce_scatter x4, waiting for transfers between devices, paired(): lax.psum_scatter(part.astype(BF), 'batch', scatter_dimension=0, tiled=True)  139 us
    unnamed x1, blocking collectives  59 us
    pallas_call x1, Pallas kernels, front(): pl.pallas_call(front_kernel, in_specs=[hbm, hbm, vmem, hbm, vmem, vmem, h...  51.1 us
    pallas_call x1, Pallas kernels, feed(): pl.pallas_call(feed_kernel, grid=(ff // tile,), in_specs=[rows, rows, row...  48.5 us
    psum x1, waiting for transfers between devices, paired(): totals = tuple((part.astype(F32) for part in lax.psum(totals, 'blk')))  32.1 us
    pallas_call x1, Pallas kernels, back(): pl.pallas_call(back_kernel, grid=(PAIRS,), in_specs=[pair] * 4 + [stat, s...  28 us
    convert_element_type x13, other arithmetic, paired(): totals = tuple((part.astype(F32) for part in lax.psum(totals, 'blk')))  17.4 us
    reshape x9, local copies, waits for them, and re-layouts, paired(): line = lambda a: a.reshape(1, -1)  11.4 us
  transfers between devices with their start and end apart: 8, of which 3 were waited for; matrix products, arithmetic and copies ran while one was open for 11% of the time, Pallas kernels for 6%

profile of v1, /device:TPU:0, one launch (start us, length us, event | category | flops | bytes accessed | tf_op | source)
XLA Modules:
  0.0 455.6 jit_solution(2993062402701018103)
XLA Ops:
  7.2 1.3 reshape.92.g2_ref
  8.5 1.3 reshape.87.g1_ref
  9.8 1.3 reshape.88.b1_ref
  11.0 1.3 reshape.89.bq_ref
  12.3 1.3 reshape.91.bout_ref
  13.6 1.3 reshape.93.b2_ref
  14.8 1.2 reshape.90.bv_ref
  16.1 1.3 reshape.95.bfc_ref
  17.4 1.3 reshape.94.bproj_ref
  18.6 51.1 %front.1 = (bf16[1024,768]{1,0:T(8,128)(2,1)}, bf16[1024,768]{1,0:T(8,128)(2,1)}, bf16[1024,768]{1,0:T(8,128)(2,1)}, bf16[1024,768]{1,0:T(8,128)(2,1)}, bf16[102...) custom-call(bf16[2,512,768]{2,1,0:T(8,128)(2,1)} %x_in.1, ...), custom_call_target="tpu_custom_call" | custom-call | tf_op jit(solution)/shard_map/front/pallas_call | solution.py:258
  69.8 48.5 %feed.1 = (bf16[1024,768]{1,0:T(8,128)(2,1)}, f32[1024,768]{1,0:T(8,128)}, bf16[1024,768]{1,0:T(8,128)(2,1)}, f32[6,2,1024]{2,1,0:T(2,128)}, bf16[768,768]{1,0:T...) custom-call(bf16[1024,768]{1,0:T(8,128)(2,1)} %get-tuple-element.38., ...), custom_call_target="tpu_custom_call" | custom-call | tf_op jit(solution)/shard_map/feed/pallas_call | solution.py:409
  118.4 0.3 convert_reduce_fusion
  118.7 0.6 fusion.14
  119.3 28.0 %back.1 = (bf16[1024,768]{1,0:T(8,128)(2,1)}, bf16[1024,768]{1,0:T(8,128)(2,1)}, bf16[1024,768]{1,0:T(8,128)(2,1)}) custom-call(bf16[1024,768]{1,0:T(8,128)(2,1)} %get-tuple-element.45.q_ref, bf16[1024,768]{1,0:T(8,128)(2,1)} %get-tuple-element.46.k_ref, bf16[1024,768]{1,0:T(8,128)(2,1)} %get-tuple-element.47.v_ref, ...), custom_call_target="tpu_custom_call" | custom-call | tf_op jit(solution)/shard_map/back/pallas_call | solution.py:498
  147.3 3.2 slice_reduce_fusion.4
  150.5 0.9 copy-done.7
  151.4 5.4 %convolution_convert_fusion = bf16[768,1920]{1,0:T(8,128)(2,1)} fusion(bf16[1024,384]{1,0:T(8,128)(2,1)S(1)} %get-tuple-element.96, bf16[1024,768]{1,0:T(8,128)(2,1)S(1)} %copy-done.10, bf16[1024,768]{1,0:T(8,128)(2,1)S(1)} %copy-done.4, bf16[1024,768]{1,0:T(8,128)(2,1)S(1)} %copy-done, f32[768]{0:T(1024)S(1)} %convert_element_type.96, ...), kind=kOutput, calls=%fused_computation.9 | convolution fusion | flops 3037888512 | bytes 8468480 | tf_op jit(solution)/shard_map/dot_general | solution.py:32
  156.9 0.7 reduce-scatter.11.cloned.1.call-update
  157.6 0.5 reduce-scatter.9.cloned.1.call-update
  158.2 7.6 %fusion.11 = (bf16[768]{0:T(1024)(128)(2,1)}, f32[1024]{0:T(1024)S(1)}, f32[1024]{0:T(1024)S(1)}, bf16[768]{0:T(1024)(128)(2,1)}, f32[1024,768]{1,0:T(8,128)S(1)}) fusion(bf16[1024,768]{1,0:T(8,128)(2,1)S(1)} %copy-done, f32[1024]{0:T(1024)S(1)} %add_rsqrt_fusion, f32[1024]{0:T(1024)S(1)} %broadcast_multiply_fusion.2, f32[768]{0:T(1024)S(1)} %convert_element_type.90, ...), kind=kOutput, calls=%fused_computation.15 | convolution fusion | flops 3039556096 | bytes 11622400 | tf_op jit(solution)/shard_map/dot_general | solution.py:28
  165.8 1.3 fusion.10
  167.1 0.9 constant_dynamic-slice_fusion.1
  168.0 2.1 collective-permute-start.1
  170.1 0.8 constant_dynamic-slice_fusion
  170.9 0.1 constant_dynamic-slice_fusion.2
  170.9 2.1 collective-permute-start
  173.0 1.7 reduce_sum.84
  174.7 0.7 convert.8
  175.5 1.2 dynamic-slice
  177.4 1.3 convert_reduce_fusion.1
  178.7 0.6 slice_reduce_fusion
  179.3 59.0 %all-reduce.9 = (bf16[768]{0:T(1024)(128)(2,1)S(1)}, bf16[768]{0:T(1024)(128)(2,1)}, bf16[768]{0:T(1024)(128)(2,1)}, bf16[384]{0:T(512)(128)(2,1)}, bf16[768]{0:...) all-reduce(bf16[768]{0:T(1024)(128)(2,1)} %get-tuple-element.60, ...), channel_id=2, replica_groups=mesh['batch'=16,'blk'=2] {'batch'}, use_global_device_ids=true, to_apply=%region_5.0.clone | all-reduce | flops 8832 | bytes 35328
  238.4 0.1 dynamic-slice.1
  238.4 0.1 dynamic-slice.11
  238.5 0.8 dynamic-slice.13
  239.9 0.8 dynamic-slice.17
  240.7 1.3 dynamic-slice.3
  241.9 1.3 dynamic-slice.5
  243.9 1.3 dynamic-slice.9
  245.1 1.3 dynamic-slice.15
  246.4 1.3 dynamic-slice.7
  247.7 5.7 %all-reduce.10 = (bf16[48]{0:T(256)(128)(2,1)}, bf16[48]{0:T(256)(128)(2,1)}, bf16[48]{0:T(256)(128)(2,1)}, bf16[24]{0:T(256)(128)(2,1)}, bf16[48]{0:T(256)(128)...) all-reduce(bf16[48]{0:T(256)(128)(2,1)S(1)} %dynamic-slice.1, ...), channel_id=1, replica_groups=mesh['batch'=16,'blk'=2] {'blk'}, use_global_device_ids=true, to_apply=%region_6.0 | all-reduce | flops 552 | bytes 2208 | tf_op jit(solution)/shard_map/psum | solution.py:586
  253.3 1.2 convert_element_type.112
  254.6 1.2 convert_element_type.100
  255.7 1.2 convert_element_type.101
  256.9 1.2 convert_element_type.104
  258.1 1.2 convert_element_type.106
  259.2 1.2 convert_element_type.108
  260.4 1.2 convert_element_type.115
  261.6 1.2 convert_element_type.93
  262.7 1.2 convert_element_type.95
  263.9 0.2 select_bitcast_fusion.5
  264.1 1.0 pad_maximum_fusion.5
  265.1 60.2 %reduce-scatter.11.cloned.1.call-done = bf16[192,768]{1,0:T(8,128)(2,1)} async-done(((bf16[3072,768]{1,0:T(8,128)(2,1)}), bf16[192,768]{1,0:T(8,128)(2,1)}) %reduce-scatter.11.cloned.1.call-update) | async-done | bytes 294928 | tf_op jit(solution)/shard_map/reduce_scatter | solution.py:583
  325.3 78.8 %reduce-scatter.9.cloned.1.call-done = bf16[48,3072]{1,0:T(8,128)(2,1)} async-done(((bf16[768,3072]{1,0:T(8,128)(2,1)}), bf16[48,3072]{1,0:T(8,128)(2,1)}) %reduce-scatter.9.cloned.1.call-update) | async-done | bytes 294928 | tf_op jit(solution)/shard_map/reduce_scatter | solution.py:583
  404.1 1.5 select_bitcast_fusion.1
  405.7 1.3 pad_maximum_fusion.4
  407.0 1.4 select_bitcast_fusion.3
  408.4 1.3 pad_maximum_fusion.3
  409.7 32.1 %all-reduce.14.cloned.1.call-done = (bf16[48,1920]{1,0:T(8,128)(2,1)}, bf16[48,768]{1,0:T(8,128)(2,1)}, bf16[48,3072]{1,0:T(8,128)(2,1)}, bf16[192,768]{1,0:T(8,128)(2,1)}) async-done(((bf16[48,1920]{1,0:T(8,128)(2,1)}, bf16[48,768]{1,0:T(8,128)(2,1)}, bf16[48,3072]{1,0:T(8,128)(2,1)}, bf16[192,768]{1,0:T(8,128)(2,1)}), (bf16[48,1920]{1,0:T(8,128)(2,1)}, bf16[48,768]{1,0:T(8,128)(2,1)}, ...) | async-done | bytes 847888 | tf_op jit(solution)/shard_map/psum | solution.py:586
  441.8 1.8 convert_element_type.109
  443.6 1.8 convert_element_type.113
  445.4 1.7 convert_element_type.99
  447.1 1.6 convert_element_type.102
  (40 shorter events, 0.3 us)
Async XLA Ops:
  7.2 257.9 %reduce-scatter.7.cloned.1.call-start = ((), (), s32[]{:S(2)}) async-start(), calls=%async_computation.5 | async-start | bytes 1253376 | tf_op jit(solution)/shard_map/reduce_scatter | solution.py:583
  69.8 48.6 %copy-start = (bf16[1024,768]{1,0:T(8,128)(2,1)S(1)}, bf16[1024,768]{1,0:T(8,128)(2,1)}, u32[]{:S(2)}) copy-start(bf16[1024,768]{1,0:T(8,128)(2,1)} %get-tuple-element.44) | copy-start | bytes 4718596
  118.3 1.0 copy-start.8
  118.3 1.0 copy-start.9
  118.3 146.8 %reduce-scatter.5.cloned.1.call-start = ((), (), s32[]{:S(2)}) async-start(), calls=%async_computation.4 | async-start | bytes 3133440 | tf_op jit(solution)/shard_map/reduce_scatter | solution.py:583
  147.3 4.1 copy-start.4
  147.3 4.1 copy-start.10
  150.5 0.9 copy-start.7
  156.8 168.4 %reduce-scatter.11.cloned.1.call-start = ((), (), s32[]{:S(2)}) async-start(), calls=%async_computation.7 | async-start | bytes 5013504 | tf_op jit(solution)/shard_map/reduce_scatter | solution.py:583
  157.6 246.5 %reduce-scatter.9.cloned.1.call-start = ((), (), s32[]{:S(2)}) async-start(), calls=%async_computation.6 | async-start | bytes 5013504 | tf_op jit(solution)/shard_map/reduce_scatter | solution.py:583
  158.1 283.6 %all-reduce.14.cloned.1.call-start = ((), (), s32[]{:S(2)}) async-start(), calls=%async_computation.8 | async-start | bytes 1695744 | tf_op jit(solution)/shard_map/psum | solution.py:586
  158.2 7.6 %copy-start.1 = (f32[1024,768]{1,0:T(8,128)S(1)}, f32[1024,768]{1,0:T(8,128)}, u32[]{:S(2)}) copy-start(f32[1024,768]{1,0:T(8,128)} %get-tuple-element.43) | copy-start | bytes 9437188
  165.8 4.3 copy-start.2
  165.8 5.1 %copy-start.5 = (bf16[1024,768]{1,0:T(8,128)(2,1)S(1)}, bf16[1024,768]{1,0:T(8,128)(2,1)}, u32[]{:S(2)}) copy-start(bf16[1024,768]{1,0:T(8,128)(2,1)} %get-tuple-element.42) | copy-start | bytes 4718596
  167.1 96.8 %copy-start.3 = (bf16[1024,384]{1,0:T(8,128)(2,1)S(1)}, bf16[1024,384]{1,0:T(8,128)(2,1)}, u32[]{:S(2)}) copy-start(bf16[1024,384]{1,0:T(8,128)(2,1)} %get-tuple-element.95) | copy-start | bytes 2359300
  168.0 236.1 %collective-permute-start.1 = (bf16[512,768]{1,0:T(8,128)(2,1)}, bf16[512,768]{1,0:T(8,128)(2,1)}, u32[]{:S(2)}, u32[]{:S(2)}) collective-permute-start(bf16[512,768]{1,0:T(8,128)(2,1)} %constant_dynamic-slice_fusion.1), channel_id=1, source_target_pairs={{0,1},{1,0},{2,3},{3,2},{4,5},{5,4},{6,7},{7,6},{8,9},{9,8},{10,11... | collective-permute-start | bytes 2359304 | tf_op jit(solution)/shard_map/ppermute | solution.py:515
  170.9 93.0 %collective-permute-start.2 = (bf16[512,384]{1,0:T(8,128)(2,1)}, bf16[512,384]{1,0:T(8,128)(2,1)S(1)}, u32[]{:S(2)}, u32[]{:S(2)}) collective-permute-start(bf16[512,384]{1,0:T(8,128)(2,1)} %constant_dynamic-slice_fusion), channel_id=1, source_target_pairs={{0,1},{1,0},{2,3},{3,2},{4,5},{5,4},{6,7},{7,6},{8,9},{9,8},{10,11... | collective-permute-start | bytes 1179656 | tf_op jit(solution)/shard_map/ppermute | solution.py:515
  170.9 236.0 %collective-permute-start = (bf16[512,768]{1,0:T(8,128)(2,1)S(1)}, bf16[512,768]{1,0:T(8,128)(2,1)}, u32[]{:S(2)}, u32[]{:S(2)}) collective-permute-start(bf16[512,768]{1,0:T(8,128)(2,1)S(1)} %constant_dynamic-slice_fusion.2), channel_id=1, source_target_pairs={{0,1},{1,0},{2,3},{3,2},{4,5},{5,4},{6,7},{7,6},{8,9},{9,8},{10,11... | collective-permute-start | bytes 2359304 | tf_op jit(solution)/shard_map/ppermute | solution.py:515
  404.1 2.8 copy-start.6
Sparse Core Ops, SparseCore 0:
  118.4 59.8 reduce-scatter.6
  182.2 64.5 reduce-scatter.4
  250.7 74.5 reduce-scatter.10
  329.5 74.5 reduce-scatter.8
  406.4 35.2 all-reduce.13
